TPU v7x, 32 devices: a whole 2x2x4 slice. The times are simulated.
32 devices in a mesh: hist: 4 (over x, core), cand: 4 (over z), fsdp: 2 (over y).
Axes of the slice: x: 2, y: 2, z: 4, core: 2. Of those that a mesh axis runs over, the one named last changes fastest.
Arguments:
- candidates: bfloat16 [256, 4, 1024], P(('hist', 'cand'), 'fsdp'), may hold values from -6 to 6
- cand_items: int32 [256, 4], replicated, may hold values from 0 to 2047, as said below
- hist_keys: bfloat16 [4, 4096, 1024], P('fsdp', 'hist'), may hold values from -6 to 6
- hist_values: bfloat16 [4, 4096, 1024], P('fsdp', 'hist'), may hold values from -6 to 6
- hist_items: int32 [4, 4096], P('fsdp', 'hist'), may hold values from 0 to 2047
- hist_buckets: int32 [4, 4096], P('fsdp', 'hist'), may hold values from 0 to 127
- lengths: int32 [4], P('fsdp'), may hold values from 1024 to 4096, as said below
- norm_gain: float32 [1024], replicated, may hold values from 0.5 to 1.5
- in_weight: bfloat16 [1024, 4096], P(None, 'fsdp'), may hold values from -0.1875 to 0.1875
- bias_table: float32 [128, 16], replicated, may hold values from -4 to 4
- out_weight: bfloat16 [1024, 1024], P(None, 'fsdp'), may hold values from -0.1875 to 0.1875
Outputs:
- scored: bfloat16 [256, 4, 1024], P(('hist', 'cand'), 'fsdp')
Inputs may be any that keep to these rules, and one draw needn't show every extreme that they name: `lengths`: history length of each user; one user of every draw has all 4096 positions. `cand_items`: item ids of the candidates, from the same catalogue as the history.
All inputs are finite; a program needn't handle non-finite values.
Results may differ from a plain program's by a relative error of at most 0.013.
Values may be sent and summed in bfloat16 or wider, within the bound.
A program may use at most 128 MiB of HBM per device.

v0:
```python
import math

import jax
import jax.numpy as jnp
from jax import lax
from jax.sharding import PartitionSpec as P


def layer_norm(values_in, epsilon):
    center = values_in - jnp.mean(values_in, axis=-1, keepdims=True)
    spread = jnp.mean(center * center, axis=-1, keepdims=True)
    return center * lax.rsqrt(spread + epsilon)


def body(
    candidates,
    cand_items,
    hist_keys,
    hist_values,
    hist_items,
    hist_buckets,
    lengths,
    norm_gain,
    in_weight,
    bias_table,
    out_weight,
):
    cand_dev, member_dev, model_width = candidates.shape
    bucket_count, head_count = bias_table.shape
    inner_width = out_weight.shape[0]
    head_dim = inner_width // head_count
    score_scale = head_dim ** (-0.5)
    hist_dev = hist_keys.shape[1]
    normed = (layer_norm(candidates.astype(jnp.float32), 1e-05) * norm_gain).astype(jnp.bfloat16)
    projected = jax.nn.silu(
        jnp.dot(
            normed,
            lax.all_gather(in_weight, "fsdp", axis=1, tiled=True),
            preferred_element_type=jnp.float32,
        )
    ).astype(jnp.bfloat16)
    gate_part = projected[:, :, :inner_width]
    value_part = projected[:, :, inner_width : 2 * inner_width]
    query_part = projected[:, :, 2 * inner_width : 3 * inner_width]
    key_part = projected[:, :, 3 * inner_width :]
    inv_len = 1.0 / (lengths.astype(jnp.float32) + 1.0)
    query_heads = query_part.astype(jnp.float32).reshape(cand_dev, member_dev, head_count, head_dim)
    own_keys = key_part.astype(jnp.float32).reshape(cand_dev, member_dev, head_count, head_dim)
    self_weight = (
        jax.nn.silu(
            jnp.sum(query_heads * own_keys, axis=-1) * score_scale + bias_table[0][None, None, :]
        )
        * inv_len[None, :, None]
    )
    self_term = (
        self_weight[..., None]
        * value_part.astype(jnp.float32).reshape(cand_dev, member_dev, head_count, head_dim)
    ).reshape(cand_dev, member_dev, inner_width)
    hist_count = lax.axis_size("hist")
    cand_count = lax.axis_size("cand")
    id_grid = cand_items.reshape(hist_count, cand_count, cand_dev, -1)
    id_mine = lax.dynamic_index_in_dim(id_grid, lax.axis_index("cand"), 1, keepdims=False)
    id_mine = lax.dynamic_slice_in_dim(id_mine, lax.axis_index("fsdp") * member_dev, member_dev, 2)
    gathered_ids = id_mine.reshape(hist_count * cand_dev, member_dev)
    one_hot = (hist_buckets[..., None] == jnp.arange(bucket_count, dtype=jnp.int32)).astype(
        jnp.float32
    )
    bias_rows = jnp.einsum("mkn,nh->mhk", one_hot, bias_table, precision=lax.Precision.HIGHEST)
    positions = lax.axis_index("hist") * hist_dev + jnp.arange(hist_dev, dtype=jnp.int32)
    live_keys = positions[None, :] < lengths[:, None]
    key_heads = hist_keys.reshape(member_dev, hist_dev, head_count, head_dim)
    value_heads = hist_values.reshape(member_dev, hist_dev, head_count, head_dim)
    gathered_queries = lax.all_gather(query_part, "hist", axis=0, tiled=True)
    row_count = cand_dev * lax.axis_size("hist")
    block_rows = math.gcd(row_count, 512)
    results = []
    for member in range(member_dev):
        query_blocks = gathered_queries[:, member].reshape(
            row_count // block_rows, block_rows, head_count, head_dim
        )
        id_blocks = gathered_ids[:, member].reshape(row_count // block_rows, block_rows)

        def one_block(block_pair):
            query_block, id_block = block_pair
            scores = jnp.einsum(
                "qhd,khd->qhk", query_block, key_heads[member], preferred_element_type=jnp.float32
            )
            scores = scores * score_scale + bias_rows[member][None]
            keep_mask = live_keys[member][None, :] & (
                hist_items[member][None, :] != id_block[:, None]
            )
            weights = jnp.where(
                keep_mask[:, None, :], jax.nn.silu(scores) * inv_len[member], 0.0
            ).astype(jnp.bfloat16)
            summed = jnp.einsum(
                "qhk,khd->qhd", weights, value_heads[member], preferred_element_type=jnp.float32
            )
            return summed.reshape(block_rows, inner_width)

        results.append(
            lax.map(one_block, (query_blocks, id_blocks)).reshape(row_count, inner_width)
        )
    attended = (
        lax.psum_scatter(
            jnp.stack(results, axis=1).astype(jnp.bfloat16), "hist", scatter_dimension=0, tiled=True
        ).astype(jnp.float32)
        + self_term
    )
    mixed = (layer_norm(attended, 1e-05) * gate_part.astype(jnp.float32)).astype(jnp.bfloat16)
    branch = jnp.dot(
        mixed,
        lax.all_gather(out_weight, "fsdp", axis=1, tiled=True),
        preferred_element_type=jnp.float32,
    )
    return (candidates.astype(jnp.float32) + branch).astype(jnp.bfloat16)


def solution(mesh):
    in_specs = (
        P(("hist", "cand"), "fsdp", None),
        P(),
        P("fsdp", "hist", None),
        P("fsdp", "hist", None),
        P("fsdp", "hist"),
        P("fsdp", "hist"),
        P("fsdp"),
        P(),
        P(None, "fsdp"),
        P(),
        P(None, "fsdp"),
    )
    out_specs = P(("hist", "cand"), "fsdp", None)
    return jax.shard_map(body, mesh=mesh, in_specs=in_specs, out_specs=out_specs, check_vma=False)
```

profile of v0, /device:TPU:0, one launch (start us, length us, event | category | flops | bytes accessed | tf_op | source)
XLA Modules:
  0.0 202.1 jit_solution(18440824670122900653)
XLA Ops:
  6.5 0.0 all-gather.3.cloned.1.call-start
  6.5 0.7 all-gather.3.cloned.1.call-update
  7.3 0.0 reduce-scatter.2.cloned.1.call-start
  7.3 0.1 reshape.157
  7.4 0.1 reshape.158
  7.5 4.0 %fusion.56 = (bf16[1,1024,1024]{2,1,0:T(8,128)(2,1)}, bf16[1,1024,1024]{2,1,0:T(8,128)(2,1)S(1)}) fusion(bf16[2,1024,1024]{2,1,0:T(8,128)(2,1)} %param.13), kind=kLoop, calls=%fused_computation.79 | loop fusion | bytes 8388608 | tf_op jit(solution)/shard_map/while/body/eval_jaxpr/slice | solution.py:86
  11.5 3.9 %copy.25 = bf16[1,1024,1024]{1,2,0:T(8,128)(2,1)} copy(bf16[1,1024,1024]{2,1,0:T(8,128)(2,1)} %get-tuple-element.45) | data formatting | bytes 4194304 | tf_op jit(solution)/shard_map/while/body/eval_jaxpr/slice | solution.py:86
  15.4 5.0 %fusion.57 = (bf16[1,1024,1024]{2,1,0:T(8,128)(2,1)}, bf16[1,1024,1024]{2,1,0:T(8,128)(2,1)}) fusion(bf16[2,1024,1024]{2,1,0:T(8,128)(2,1)} %param.14), kind=kLoop, calls=%fused_computation.80 | loop fusion | bytes 8388608 | tf_op jit(solution)/shard_map/while/body/eval_jaxpr/slice | solution.py:96
  20.4 4.2 %copy.27 = bf16[1,1024,1024]{1,2,0:T(8,128)(2,1)} copy(bf16[1,1024,1024]{2,1,0:T(8,128)(2,1)} %get-tuple-element.47) | data formatting | bytes 4194304 | tf_op jit(solution)/shard_map/while/body/eval_jaxpr/slice | solution.py:96
  24.6 0.0 copy-start.7
  24.6 0.0 copy-start.2
  24.6 2.6 %copy.29 = bf16[1,1024,1024]{1,2,0:T(8,128)(2,1)} copy(bf16[1,1024,1024]{2,1,0:T(8,128)(2,1)S(1)} %get-tuple-element.46) | data formatting | bytes 4194304 | tf_op jit(solution)/shard_map/while/body/eval_jaxpr/slice | solution.py:86
  27.2 4.0 %copy.31 = bf16[1,1024,1024]{1,2,0:T(8,128)(2,1)} copy(bf16[1,1024,1024]{2,1,0:T(8,128)(2,1)} %get-tuple-element.48) | data formatting | bytes 4194304 | tf_op jit(solution)/shard_map/while/body/eval_jaxpr/slice | solution.py:96
  31.2 0.6 fusion.60
  31.8 0.1 broadcast_compare_fusion
  31.9 0.1 convert_reduce_fusion
  32.0 0.2 fusion.37
  32.2 0.2 compare_and_fusion
  32.4 0.0 copy-done.4
  32.4 0.0 copy-done.7
  32.4 0.9 convolution_bitcast_fusion
  33.4 82.3 %all-gather.3.cloned.1.call-done = bf16[1024,4096]{1,0:T(8,128)(2,1)} async-done(((bf16[1024,2048]{1,0:T(8,128)(2,1)}), bf16[1024,4096]{1,0:T(8,128)(2,1)}) %all-gather.3.cloned.1.call-update) | async-done | bytes 8388624 | tf_op jit(solution)/shard_map/all_gather | solution.py:38
  115.6 5.0 %multiply_convert_fusion = bf16[16,2,4096]{2,0,1:T(8,128)(2,1)S(1)} fusion(bf16[1024,4096]{1,0:T(8,128)(2,1)} %all-gather.3.cloned.1.call-done, f32[1024]{0:T(1024)S(1)} %copy-done.2, f32[16,2]{0,1:T(2,128)S(1)} %add_rsqrt_fusion.1, f32[16,2]{0,1:T(2,128)S(1)} %broadcast_multiply_fusion.1, bf16[16,2,1024]{2,1,0:T(2,128)(2,1)S(1)} %copy-done.1), kind=kOutput, calls=%fused_computation.31 | convolution fusion | flops 269254656 | bytes 8720640 | tf_op jit(solution)/shard_map/dot_general | solution.py:36
  120.7 5.8 %all_gather.10 = bf16[64,2,1024]{2,0,1:T(8,128)(2,1)S(1)} all-gather(bf16[16,2,1024]{2,0,1:T(8,128)(2,1)S(1)} %slice.101), channel_id=1, replica_groups=mesh['hist'=4,'cand'=4,'fsdp'=2] {'hist'}, dimensions={0}, use_global_device_ids=true | all-gather | bytes 327680 | tf_op jit(solution)/shard_map/all_gather | solution.py:73
  126.5 0.2 squeeze.40
  126.7 5.1 %fusion.21 = bf16[64,16,64]{2,0,1:T(8,128)(2,1)S(1)} fusion(bf16[1024,16,64]{0,2,1:T(8,128)(2,1)} %bitcast.105, bf16[1024,16,64]{0,2,1:T(8,128)(2,1)} %bitcast.104, f32[]{:T(128)} %bitcast.8, f32[16,1024]{1,0:T(8,128)S(1)} %get-tuple-element.61, pred[64,1024]{1,0:T(8,128)(4,1)S(1)} %get-tuple-element.80, bf16[64,16,64]{2,1,0:T(8,128)(2,1)S(1)} %squeeze.40), kind=kOutput, calls=%fused_computation.25 | convolution fusion | flops 277938176 | bytes 4587524 | tf_op jit(solution)/shard_map/while/body/eval_jaxpr/qhk,khd->qhd/dot_general | solution.py:95
  131.7 0.2 copy.28
  131.9 0.2 stack_reshape.8
  132.1 0.2 squeeze.44
  132.3 4.2 %fusion.20 = bf16[64,16,64]{2,0,1:T(8,128)(2,1)S(1)} fusion(bf16[1024,16,64]{0,2,1:T(8,128)(2,1)} %bitcast.103, bf16[1024,16,64]{0,2,1:T(8,128)(2,1)S(1)} %bitcast.102, f32[]{:T(128)} %bitcast.16, f32[16,1024]{1,0:T(8,128)S(1)} %get-tuple-element.62, pred[64,1024]{1,0:T(8,128)(4,1)S(1)} %get-tuple-element.69, bf16[64,16,64]{2,1,0:T(8,128)(2,1)S(1)} %squeeze.44), kind=kOutput, calls=%fused_computation.24 | convolution fusion | flops 277938176 | bytes 4587524 | tf_op jit(solution)/shard_map/while/body/eval_jaxpr/qhk,khd->qhd/dot_general | solution.py:95
  136.5 0.2 copy.32
  136.7 0.2 stack_reshape.9
  136.9 0.8 pad_maximum_fusion
  137.7 0.0 reduce-scatter.2.cloned.1.call-update
  137.7 0.0 all-gather.5.cloned.1.call-start
  137.8 0.7 all-gather.5.cloned.1.call-update
  138.4 0.1 slice_reduce_fusion.2
  138.6 0.1 mul.142
  138.7 0.1 reduce_sum.47
  138.8 0.1 multiply_multiply_fusion
  138.9 0.1 mul.148
  139.0 0.1 mul.149
  139.2 18.7 %reduce-scatter.2.cloned.1.call-done = bf16[16,2,1024]{2,0,1:T(8,128)(2,1)} async-done(((bf16[64,2,1024]{2,0,1:T(8,128)(2,1)}), bf16[16,2,1024]{2,0,1:T(8,128)(2,1)}) %reduce-scatter.2.cloned.1.call-update) | async-done | bytes 65552 | tf_op jit(solution)/shard_map/reduce_scatter | solution.py:104
  157.9 0.9 fusion.55
  158.8 1.0 multiply_reduce_fusion
  159.9 32.8 %all-gather.5.cloned.1.call-done = bf16[1024,1024]{1,0:T(8,128)(2,1)} async-done(((bf16[1024,512]{1,0:T(8,128)(2,1)}), bf16[1024,1024]{1,0:T(8,128)(2,1)}) %all-gather.5.cloned.1.call-update) | async-done | bytes 2097168 | tf_op jit(solution)/shard_map/all_gather | solution.py:112
  192.7 2.1 %fusion.25 = bf16[16,2,1024]{2,0,1:T(8,128)(2,1)S(1)} fusion(bf16[1024,1024]{1,0:T(8,128)(2,1)} %all-gather.5.cloned.1.call-done, bf16[16,2,4096]{2,0,1:T(8,128)(2,1)S(1)} %multiply_convert_fusion, f32[16,2]{0,1:T(2,128)S(1)} %add_rsqrt_fusion, f32[16,2]{0,1:T(2,128)S(1)} %broadcast_multiply_fusion, bf16[16,2,1024]{2,1,0:T(2,128)(2,1)S(1)} %copy-done.1, ...), kind=kOutput, calls=%fused_computation.28 | convolution fusion | flops 67502080 | bytes 2557952 | tf_op jit(solution)/shard_map/dot_general | solution.py:110
  194.8 0.7 copy.33
  (26 shorter events, 0.2 us)
Async XLA Ops:
  6.5 0.8 copy-start.5
  6.5 109.1 %all-gather.3.cloned.1.call-start = ((), (), s32[]{:S(2)}) async-start(), calls=%async_computation.1 | async-start | bytes 12582912 | tf_op jit(solution)/shard_map/all_gather | solution.py:38
  7.3 150.6 %reduce-scatter.2.cloned.1.call-start = ((), (), s32[]{:S(2)}) async-start(), calls=%async_computation.2 | async-start | bytes 327680 | tf_op jit(solution)/shard_map/reduce_scatter | solution.py:104
  24.6 6.7 %copy-start.6 = (s32[2]{0:T(128)S(1)}, s32[2]{0:T(128)}, u32[]{:S(2)}) copy-start(s32[2]{0:T(128)} %param.17) | copy-start | bytes 28
  24.6 7.4 %copy-start.1 = (bf16[16,2,1024]{2,1,0:T(2,128)(2,1)S(1)}, bf16[16,2,1024]{2,1,0:T(2,128)(2,1)}, u32[]{:S(2)}) copy-start(bf16[16,2,1024]{2,1,0:T(2,128)(2,1)} %param.11) | copy-start | bytes 196612
  24.6 7.7 %copy-start.3 = (s32[2,1024]{1,0:T(2,128)S(1)}, s32[2,1024]{1,0:T(2,128)}, u32[]{:S(2)}) copy-start(s32[2,1024]{1,0:T(2,128)} %param.15) | copy-start | bytes 24580
  24.6 7.8 %copy-start.4 = (f32[128,16]{0,1:T(8,128)S(1)}, f32[128,16]{0,1:T(8,128)}, u32[]{:S(2)}) copy-start(f32[128,16]{0,1:T(8,128)} %param.20) | copy-start | bytes 24580
  24.6 7.8 %copy-start.7 = (s32[2,1024]{1,0:T(2,128)S(1)}, s32[2,1024]{1,0:T(2,128)}, u32[]{:S(2)}) copy-start(s32[2,1024]{1,0:T(2,128)} %param.16) | copy-start | bytes 24580
  24.6 91.1 %copy-start.2 = (f32[1024]{0:T(1024)S(1)}, f32[1024]{0:T(1024)}, u32[]{:S(2)}) copy-start(f32[1024]{0:T(1024)} %param.18) | copy-start | bytes 12292
  126.7 5.6 %copy-start = (bf16[1,1024,1024]{1,2,0:T(8,128)(2,1)S(1)}, bf16[1,1024,1024]{1,2,0:T(8,128)(2,1)}, u32[]{:S(2)}) copy-start(bf16[1,1024,1024]{1,2,0:T(8,128)(2,1)} %copy.29) | copy-start | bytes 6291460
  137.7 55.0 %all-gather.5.cloned.1.call-start = ((), (), s32[]{:S(2)}) async-start(), calls=%async_computation.3 | async-start | bytes 3145728 | tf_op jit(solution)/shard_map/all_gather | solution.py:112
Sparse Core Ops, SparseCore 0:
  8.9 106.6 all-gather.2
  137.8 20.0 reduce-scatter.1
  159.5 33.1 all-gather.4
where the time goes:
time: 203 us; the launch traced here: 202 us
  waiting for transfers between devices  135 us (67%)
  local copies, waits for them, and re-layouts  26.8 us (13%)
  matrix products  17.4 us (9%)
  between operations  13.4 us (7%)
  blocking collectives  5.79 us (3%)
  other arithmetic  3.45 us (2%)
    all_gather x1, waiting for transfers between devices, body(): lax.all_gather(in_weight, 'fsdp', axis=1, tiled=True)  82.3 us
    all_gather x1, waiting for transfers between devices, body(): lax.all_gather(out_weight, 'fsdp', axis=1, tiled=True)  32.8 us
    reduce_scatter x1, waiting for transfers between devices, body(): lax.psum_scatter(jnp.stack(results, axis=1).astype(jnp.bfloat16), 'hist',...  18.7 us
    slice x3, local copies, waits for them, and re-layouts, one_block(): value_heads[member]  13.2 us
    slice x3, local copies, waits for them, and re-layouts, one_block(): key_heads[member]  10.5 us
    dot_general x2, matrix products, one_block(): jnp.einsum('qhk,khd->qhd', weights, value_heads[member], preferred_elemen...  9.27 us
    all_gather x1, blocking collectives, body(): gathered_queries = lax.all_gather(query_part, 'hist', axis=0, tiled=True)  5.79 us
    dot_general x1, matrix products, body(): jnp.dot(normed, lax.all_gather(in_weight, 'fsdp', axis=1, tiled=True), pr...  5.01 us
  transfers between devices with their start and end apart: 3, of which 3 were waited for; matrix products, arithmetic and copies ran while one was open for 14% of the time, Pallas kernels for 0%

commit v1 on v0

v1 whole, which is shorter than its diff:
```python
import functools

import jax
import jax.numpy as jnp
from jax import lax
from jax.experimental import pallas as pl
from jax.experimental.pallas import tpu as pltpu
from jax.sharding import PartitionSpec as P

MESH = pl.DeviceIdType.MESH
F32 = jnp.float32
BF16 = jnp.bfloat16
NT = (((1,), (1,)), ((), ()))


def half_silu(u):
    return u + u * jnp.tanh(u)


def layer_norm(x):
    c = x - jnp.mean(x, axis=-1, keepdims=True)
    return c * lax.rsqrt(jnp.mean(c * c, axis=-1, keepdims=True) + 1e-05)


def kernel(
    hist_n,
    cand_n,
    cand_ref,
    ids_ref,
    keys_hbm,
    vals_hbm,
    items_ref,
    buckets_ref,
    len_ref,
    gain_ref,
    inw_hbm,
    table_ref,
    outw_hbm,
    out_ref,
    inw,
    outw,
    keys,
    vals,
    x_buf,
    proj,
    psend,
    gq,
    part,
    recv,
    hbias,
    keep,
    mix,
    branch,
    bsend,
    loc_sem,
    a_send,
    a_recv,
    c_send,
    c_recv,
    d_send,
    d_recv,
    f_send,
    f_recv,
    m_send,
    m_recv,
    b_send,
    b_recv,
):
    hist = lax.axis_index("hist")
    cand = lax.axis_index("cand")
    fsdp = lax.axis_index("fsdp")
    other = 1 - fsdp
    members, cdev, width = cand_ref.shape
    heads, buckets = table_ref.shape
    inner = part.shape[-1]
    rows_own = members * cdev
    key_n = keys.shape[1]
    rows = hist_n * cdev
    hd = inner // heads
    group = 256 // hd
    gcols = group * hd
    group_n = inner // gcols

    def remote(src, dst, ssem, rsem, **where):
        return pltpu.make_async_remote_copy(
            src_ref=src, dst_ref=dst, send_sem=ssem, recv_sem=rsem, device_id=where, device_id_type=MESH
        )

    loc = [pltpu.make_async_copy(inw_hbm, inw, loc_sem.at[0])]
    for m in range(members):
        loc.append(pltpu.make_async_copy(keys_hbm.at[m], keys.at[m], loc_sem.at[1 + 2 * m]))
        loc.append(pltpu.make_async_copy(vals_hbm.at[m], vals.at[m], loc_sem.at[2 + 2 * m]))
    loc.append(pltpu.make_async_copy(outw_hbm, outw, loc_sem.at[1 + 2 * members]))

    barrier = pltpu.get_barrier_semaphore()
    peers = [lax.rem(hist + o, hist_n) for o in range(1, hist_n)]
    for peer in peers:
        pl.semaphore_signal(barrier, inc=1, device_id={"hist": peer}, device_id_type=MESH)
    pl.semaphore_signal(barrier, inc=1, device_id={"fsdp": other}, device_id_type=MESH)
    for copy in loc:
        copy.start()
    x = cand_ref[...].astype(F32).reshape(rows_own, width)
    x_buf[0] = (layer_norm(x) * gain_ref[...]).astype(BF16)
    pl.semaphore_wait(barrier, hist_n)

    a_copy = remote(x_buf.at[0], x_buf.at[1], a_send, a_recv, fsdp=other)
    a_copy.start()

    table = table_ref[...]
    t_hi = table.astype(BF16)
    rest = table - t_hi.astype(F32)
    t_mid = rest.astype(BF16)
    t_lo = (rest - t_mid.astype(F32)).astype(BF16)
    t3 = jnp.concatenate([t_hi, t_mid, t_lo], axis=0)
    for m in range(members):
        one_hot = (
            lax.broadcasted_iota(jnp.int32, (buckets, key_n), 0) == buckets_ref[m : m + 1, :]
        )
        b3 = jnp.dot(t3, one_hot.astype(F32).astype(BF16), preferred_element_type=F32)
        hbias[m] = 0.5 * (b3[:heads] + b3[heads : 2 * heads] + b3[2 * heads :])

    loc[0].wait()
    a_copy.wait()
    xs = x_buf[...].reshape(2 * rows_own, width)

    def project(p):
        u = 0.5 * jnp.dot(xs, inw[:, p * inner : (p + 1) * inner], preferred_element_type=F32)
        y = half_silu(u).astype(BF16)
        proj[2 * fsdp + p] = y[:rows_own].reshape(members, cdev, inner)
        psend[p] = y[rows_own:].reshape(members, cdev, inner)
        copy = remote(psend.at[p], proj.at[2 * fsdp + p], c_send.at[p], c_recv.at[p], fsdp=other)
        copy.start()
        return copy

    c0 = project(0)
    c1 = project(1)
    c0.wait()
    d_copies = [
        remote(proj.at[2], gq.at[hist], d_send.at[o], d_recv.at[o], hist=peer)
        for o, peer in enumerate(peers)
    ]
    for copy in d_copies:
        copy.start()
    gq[hist] = proj[2]

    lane_ids = lax.broadcasted_iota(jnp.int32, (cdev, ids_ref.shape[1]), 1)
    place = hist * key_n + lax.broadcasted_iota(jnp.int32, (1, key_n), 1)
    for m in range(members):
        length = jnp.full((1, key_n), len_ref[m], jnp.int32)
        scale = jnp.where(place < length, 1.0 / (length.astype(F32) + 1.0), 0.0)

        def fill(h, carry):
            block = ids_ref[pl.ds(pl.multiple_of((h * cand_n + cand) * cdev, cdev), cdev), :]
            mine = jnp.sum(
                jnp.where(lane_ids == fsdp * members + m, block, 0), axis=1, keepdims=True
            )
            keep[m, h] = jnp.where(mine != items_ref[m : m + 1, :], scale, 0.0)
            return carry

        lax.fori_loop(0, hist_n, fill, 0)

    for copy in d_copies:
        copy.wait()

    hb = 4 if hist_n % 4 == 0 else 1
    rb = hb * cdev
    lane_head = lax.broadcasted_iota(jnp.int32, (rb, gcols), 1) // hd
    f_copies = []
    chunk = min(key_n, 512)
    for m in range(members):
        loc[1 + 2 * m].wait()
        loc[2 + 2 * m].wait()

        def step(i, carry):
            r = i // group_n
            g = i % group_n
            cols = pl.ds(pl.multiple_of(g * gcols, gcols), gcols)
            hs = pl.ds(r * hb, hb)
            q = gq[hs, m, :, cols].reshape(rb, gcols).astype(F32) * (0.5 * hd ** (-0.5))
            q4 = jnp.concatenate(
                [jnp.where(lane_head == h, q, 0.0).astype(BF16) for h in range(group)], axis=0
            )
            total = jnp.zeros((group * rb, gcols), F32)
            for j in range(0, key_n, chunk):
                s = lax.dot_general(
                    q4, keys[m, pl.ds(j, chunk), cols], NT, preferred_element_type=F32
                )
                kp = keep[m, hs, :, pl.ds(j, chunk)].reshape(rb, chunk)
                ws = []
                for h in range(group):
                    u = s[h * rb : (h + 1) * rb] + hbias[m, pl.ds(g * group + h, 1), pl.ds(j, chunk)]
                    ws.append((half_silu(u) * kp).astype(BF16))
                total += jnp.dot(
                    jnp.concatenate(ws, axis=0),
                    vals[m, pl.ds(j, chunk), cols],
                    preferred_element_type=F32,
                )
            summed = jnp.where(lane_head == 0, total[:rb], 0.0)
            for h in range(1, group):
                summed += jnp.where(lane_head == h, total[h * rb : (h + 1) * rb], 0.0)
            part[m, hs, :, cols] = summed.astype(BF16).reshape(hb, cdev, gcols)
            return carry

        lax.fori_loop(0, (hist_n // hb) * group_n, step, 0)
        for o, peer in enumerate(peers):
            copy = remote(
                part.at[m, peer], recv.at[m, hist], f_send.at[m, o], f_recv.at[m, o], hist=peer
            )
            copy.start()
            f_copies.append(copy)

    c1.wait()
    blk = (
        lax.broadcasted_iota(jnp.int32, (gcols, gcols), 0) // hd
        == lax.broadcasted_iota(jnp.int32, (gcols, gcols), 1) // hd
    ).astype(F32).astype(BF16)
    prod = proj[2].astype(F32).reshape(rows_own, inner) * proj[3].astype(F32).reshape(rows_own, inner)
    p_hi = prod.astype(BF16)
    p_lo = (prod - p_hi.astype(F32)).astype(BF16)
    dots = jnp.concatenate(
        [
            jnp.dot(p_hi[:, c : c + gcols], blk, preferred_element_type=F32)
            + jnp.dot(p_lo[:, c : c + gcols], blk, preferred_element_type=F32)
            for c in range(0, inner, gcols)
        ],
        axis=1,
    )
    lane = lax.broadcasted_iota(jnp.int32, (heads, inner), 1) // hd
    bias0 = jnp.sum(
        jnp.where(lax.broadcasted_iota(jnp.int32, (heads, inner), 0) == lane, table[:, 0:1], 0.0),
        axis=0,
        keepdims=True,
    )
    own = half_silu(dots * (0.5 * hd ** (-0.5)) + 0.5 * bias0)
    own = own * proj[1].astype(F32).reshape(rows_own, inner)
    inv = jnp.concatenate(
        [1.0 / (jnp.full((cdev, inner), len_ref[m], jnp.int32).astype(F32) + 1.0) for m in range(members)],
        axis=0,
    )
    attended = own * inv
    for m in range(members):
        recv[m, hist] = part[m, hist]
    for copy in f_copies:
        copy.wait()
    attended += jnp.sum(recv[...].astype(F32), axis=1).reshape(rows_own, inner)
    mix[0] = (layer_norm(attended) * proj[0].astype(F32).reshape(rows_own, inner)).astype(BF16)
    m_copy = remote(mix.at[0], mix.at[1], m_send, m_recv, fsdp=other)
    m_copy.start()
    loc[-1].wait()
    m_copy.wait()
    bsend[...] = jnp.dot(mix[1], outw[...], preferred_element_type=F32)
    b_copy = remote(bsend, branch.at[fsdp], b_send, b_recv, fsdp=other)
    b_copy.start()
    branch[fsdp] = jnp.dot(mix[0], outw[...], preferred_element_type=F32)
    b_copy.wait()
    full = jnp.concatenate([branch[0], branch[1]], axis=1)
    x = cand_ref[...].astype(F32).reshape(rows_own, width)
    out_ref[...] = (x + full).astype(BF16).reshape(members, cdev, width)


def body(
    hist_n,
    cand_n,
    candidates,
    cand_items,
    hist_keys,
    hist_values,
    hist_items,
    hist_buckets,
    lengths,
    norm_gain,
    in_weight,
    bias_table,
    out_weight,
):
    cdev, members, width = candidates.shape
    key_n = hist_keys.shape[1]
    inner = out_weight.shape[0]
    heads = bias_table.shape[1]
    own = members * cdev
    vmem = pl.BlockSpec(memory_space=pltpu.VMEM)
    hbm = pl.BlockSpec(memory_space=pl.ANY)
    smem = pl.BlockSpec(memory_space=pltpu.SMEM)
    dma = pltpu.SemaphoreType.DMA
    peers = max(hist_n - 1, 1)
    out = pl.pallas_call(
        functools.partial(kernel, hist_n, cand_n),
        out_shape=jax.ShapeDtypeStruct((members, cdev, width), BF16),
        in_specs=[vmem, vmem, hbm, hbm, vmem, vmem, smem, vmem, hbm, vmem, hbm],
        out_specs=vmem,
        scratch_shapes=[
            pltpu.VMEM(in_weight.shape, BF16),
            pltpu.VMEM(out_weight.shape, BF16),
            pltpu.VMEM(hist_keys.shape, BF16),
            pltpu.VMEM(hist_values.shape, BF16),
            pltpu.VMEM((2, own, width), BF16),
            pltpu.VMEM((4, members, cdev, inner), BF16),
            pltpu.VMEM((2, members, cdev, inner), BF16),
            pltpu.VMEM((hist_n, members, cdev, inner), BF16),
            pltpu.VMEM((members, hist_n, cdev, inner), BF16),
            pltpu.VMEM((members, hist_n, cdev, inner), BF16),
            pltpu.VMEM((members, heads, key_n), F32),
            pltpu.VMEM((members, hist_n, cdev, key_n), F32),
            pltpu.VMEM((2, own, inner), BF16),
            pltpu.VMEM((2, own, out_weight.shape[1]), F32),
            pltpu.VMEM((own, out_weight.shape[1]), F32),
            dma((2 + 2 * members,)),
            dma(()),
            dma(()),
            dma((2,)),
            dma((2,)),
            dma((peers,)),
            dma((peers,)),
            dma((members, peers)),
            dma((members, peers)),
            dma(()),
            dma(()),
            dma(()),
            dma(()),
        ],
        compiler_params=pltpu.CompilerParams(
            collective_id=0, has_side_effects=True, vmem_limit_bytes=56 * 1024 * 1024
        ),
    )(
        candidates.transpose(1, 0, 2),
        cand_items,
        hist_keys,
        hist_values,
        hist_items,
        hist_buckets,
        lengths,
        norm_gain.reshape(1, width),
        in_weight,
        bias_table.T,
        out_weight,
    )
    return out.transpose(1, 0, 2)


def solution(mesh):
    in_specs = (
        P(("hist", "cand"), "fsdp", None),
        P(),
        P("fsdp", "hist", None),
        P("fsdp", "hist", None),
        P("fsdp", "hist"),
        P("fsdp", "hist"),
        P("fsdp"),
        P(),
        P(None, "fsdp"),
        P(),
        P(None, "fsdp"),
    )
    out_specs = P(("hist", "cand"), "fsdp", None)
    return jax.shard_map(
        functools.partial(body, mesh.shape["hist"], mesh.shape["cand"]),
        mesh=mesh,
        in_specs=in_specs,
        out_specs=out_specs,
        check_vma=False,
    )
```

time: 203 us -> 36.8 us (0.18)
  waiting for transfers between devices: 135 us -> 0 us
  Pallas kernels: 0 us -> 32 us
  local copies, waits for them, and re-layouts: 26.8 us -> 4.48 us
  matrix products: 17.4 us -> 0 us
  between operations: 13.4 us -> 0.01 us
  blocking collectives: 5.79 us -> 0 us
  other arithmetic: 3.45 us -> 0 us
    all_gather x2 -> x0, waiting for transfers between devices: 115 us -> none  [the longest x1 82.3 us: body(): lax.all_gather(in_weight, 'fsdp', axis=1, tiled=True)]
    pallas_call x0 -> x1, Pallas kernels: none -> 32 us  [body(): pl.pallas_call(functools.partial(kernel, hist_n, cand_n), out_shape=jax.S...]
    slice x12 -> x0, local copies, waits for them, and re-layouts: 24.4 us -> none  [the longest x3 13.2 us: one_block(): value_heads[member]]
    reduce_scatter x1 -> x0, waiting for transfers between devices: 18.7 us -> none  [body(): lax.psum_scatter(jnp.stack(results, axis=1).astype(jnp.bfloat16), 'hist',...]
    dot_general x5 -> x0, matrix products: 17.4 us -> none  [the longest x2 9.27 us: one_block(): jnp.einsum('qhk,khd->qhd', weights, value_heads[member], preferred_elemen...]
    all_gather x1 -> x0, blocking collectives: 5.79 us -> none  [body(): gathered_queries = lax.all_gather(query_part, 'hist', axis=0, tiled=True)]
    unnamed x16 -> x2, local copies, waits for them, and re-layouts: 0.04 us -> 2.94 us
    reduce_sum x5 -> x0, other arithmetic: 2.36 us -> none  [the longest x2 1.18 us: layer_norm(): spread = jnp.mean(center * center, axis=-1, keepdims=True)]
  transfers between devices with their start and end apart: 3 -> 0, of which waited for: 3 -> 0; matrix products, arithmetic and copies ran while one was open for 14% -> 0% of each run, Pallas kernels for 0% -> 0%
where the time goes in v1:
time: 36.8 us; the launch traced here: 36.5 us
  Pallas kernels  32 us (87%)
  local copies, waits for them, and re-layouts  4.48 us (12%)
    pallas_call x1, Pallas kernels, body(): pl.pallas_call(functools.partial(kernel, hist_n, cand_n), out_shape=jax.S...  32 us
    unnamed x2, local copies, waits for them, and re-layouts  2.94 us
    transpose x1, local copies, waits for them, and re-layouts, body(): return out.transpose(1, 0, 2)  1.54 us

profile of v1, /device:TPU:0, one launch (start us, length us, event | category | flops | bytes accessed | tf_op | source)
XLA Modules:
  0.0 36.5 jit_solution(626621471685226626)
XLA Ops:
  0.0 1.5 %copy.16 = bf16[16,2,1024]{2,0,1:T(8,128)(2,1)} copy(bf16[16,2,1024]{2,1,0:T(2,128)(2,1)} %param.11) | data formatting | bytes 131072 | tf_op args[0]
  1.5 1.5 %copy.13.ids_ref = s32[256,4]{1,0:T(8,128)} copy(s32[256,4]{0,1:T(4,128)} %param.12) | data formatting | bytes 8192 | tf_op args[1]
  2.9 32.0 %shard_map.109 = bf16[2,16,1024]{2,1,0:T(8,128)(2,1)} custom-call(bf16[2,16,1024]{2,1,0:T(8,128)(2,1)} %bitcast.7, s32[256,4]{1,0:T(8,128)} %copy.13.ids_ref, bf16[2,1024,1024]{2,1,0:T(8,128)(2,1)} %keys_hbm.1, bf16[2,1024,1024]{2,1,0:T(8,128)(2,1)} %vals_hbm.1, s32[2,1024]{1,0:T(2,128)} %items_ref.1, s32[2,1024]{1,0:T(2,128)} %buckets_ref.1, s32[2]{0:T(128)} %len_ref.1, ...), custom_call_target="tpu_custom_call" | custom-call | tf_op jit(solution)/shard_map/pallas_call | solution.py:286
  35.0 1.5 %copy.14 = bf16[16,2,1024]{2,1,0:T(2,128)(2,1)} copy(bf16[16,2,1024]{2,0,1:T(8,128)(2,1)} %bitcast.6) | data formatting | bytes 131072 | tf_op jit(solution)/shard_map/transpose | solution.py:337

commit v2 on v1

--- a/solution.py
+++ b/solution.py
@@ -49,9 +49,6 @@
     recv,
     hbias,
     keep,
-    mix,
-    branch,
-    bsend,
     loc_sem,
     a_send,
     a_recv,
@@ -61,21 +58,20 @@
     d_recv,
     f_send,
     f_recv,
-    m_send,
-    m_recv,
-    b_send,
-    b_recv,
+    o_send,
+    o_recv,
+    s_send,
+    s_recv,
 ):
     hist = lax.axis_index("hist")
     cand = lax.axis_index("cand")
     fsdp = lax.axis_index("fsdp")
     other = 1 - fsdp
-    members, cdev, width = cand_ref.shape
+    cdev, members, width = cand_ref.shape
     heads, buckets = table_ref.shape
     inner = part.shape[-1]
     rows_own = members * cdev
     key_n = keys.shape[1]
-    rows = hist_n * cdev
     hd = inner // heads
     group = 256 // hd
     gcols = group * hd
@@ -90,7 +86,8 @@
     for m in range(members):
         loc.append(pltpu.make_async_copy(keys_hbm.at[m], keys.at[m], loc_sem.at[1 + 2 * m]))
         loc.append(pltpu.make_async_copy(vals_hbm.at[m], vals.at[m], loc_sem.at[2 + 2 * m]))
-    loc.append(pltpu.make_async_copy(outw_hbm, outw, loc_sem.at[1 + 2 * members]))
+    w_copy = pltpu.make_async_copy(outw_hbm, outw.at[fsdp], loc_sem.at[1 + 2 * members])
+    loc.insert(1, w_copy)
 
     barrier = pltpu.get_barrier_semaphore()
     peers = [lax.rem(hist + o, hist_n) for o in range(1, hist_n)]
@@ -99,7 +96,8 @@
     pl.semaphore_signal(barrier, inc=1, device_id={"fsdp": other}, device_id_type=MESH)
     for copy in loc:
         copy.start()
-    x = cand_ref[...].astype(F32).reshape(rows_own, width)
+    x3 = cand_ref[...].astype(F32)
+    x = jnp.concatenate([x3[:, m, :] for m in range(members)], axis=0)
     x_buf[0] = (layer_norm(x) * gain_ref[...]).astype(BF16)
     pl.semaphore_wait(barrier, hist_n)
 
@@ -126,41 +124,63 @@
     def project(p):
         u = 0.5 * jnp.dot(xs, inw[:, p * inner : (p + 1) * inner], preferred_element_type=F32)
         y = half_silu(u).astype(BF16)
+        psend[p] = y[rows_own:].reshape(members, cdev, inner)
+        copies = []
+        for m in range(members):
+            copy = remote(
+                psend.at[p, m],
+                proj.at[2 * fsdp + p, m],
+                c_send.at[p, m],
+                c_recv.at[p, m],
+                fsdp=other,
+            )
+            copy.start()
+            copies.append(copy)
         proj[2 * fsdp + p] = y[:rows_own].reshape(members, cdev, inner)
-        psend[p] = y[rows_own:].reshape(members, cdev, inner)
-        copy = remote(psend.at[p], proj.at[2 * fsdp + p], c_send.at[p], c_recv.at[p], fsdp=other)
-        copy.start()
-        return copy
+        return copies
 
     c0 = project(0)
-    c1 = project(1)
-    c0.wait()
-    d_copies = [
-        remote(proj.at[2], gq.at[hist], d_send.at[o], d_recv.at[o], hist=peer)
-        for o, peer in enumerate(peers)
-    ]
-    for copy in d_copies:
-        copy.start()
-    gq[hist] = proj[2]
 
     lane_ids = lax.broadcasted_iota(jnp.int32, (cdev, ids_ref.shape[1]), 1)
+    row_ids = lax.broadcasted_iota(jnp.int32, (cdev, ids_ref.shape[1]), 0)
     place = hist * key_n + lax.broadcasted_iota(jnp.int32, (1, key_n), 1)
     for m in range(members):
         length = jnp.full((1, key_n), len_ref[m], jnp.int32)
         scale = jnp.where(place < length, 1.0 / (length.astype(F32) + 1.0), 0.0)
 
         def fill(h, carry):
-            block = ids_ref[pl.ds(pl.multiple_of((h * cand_n + cand) * cdev, cdev), cdev), :]
+            ids = ids_ref[pl.ds(fsdp * members + m, 1), :]
             mine = jnp.sum(
-                jnp.where(lane_ids == fsdp * members + m, block, 0), axis=1, keepdims=True
+                jnp.where(lane_ids == row_ids + (h * cand_n + cand) * cdev, ids, 0),
+                axis=1,
+                keepdims=True,
             )
             keep[m, h] = jnp.where(mine != items_ref[m : m + 1, :], scale, 0.0)
             return carry
 
         lax.fori_loop(0, hist_n, fill, 0)
 
-    for copy in d_copies:
-        copy.wait()
+    d_copies = []
+    for m in range(members):
+        c0[m].wait()
+        d_copies.append(
+            [
+                remote(
+                    proj.at[2, m], gq.at[m, hist], d_send.at[m, o], d_recv.at[m, o], hist=peer
+                )
+                for o, peer in enumerate(peers)
+            ]
+        )
+        for copy in d_copies[m]:
+            copy.start()
+        gq[m, hist] = proj[2, m]
+    c1 = project(1)
+
+    depth = inner // 2
+    rows = pl.ds(pl.multiple_of(lax.rem(hist, 2) * depth, depth), depth)
+    w_copy.wait()
+    o_copy = remote(outw.at[fsdp, rows], outw.at[fsdp, rows], o_send, o_recv, fsdp=other)
+    o_copy.start()
 
     hb = 4 if hist_n % 4 == 0 else 1
     rb = hb * cdev
@@ -168,15 +188,17 @@
     f_copies = []
     chunk = min(key_n, 512)
     for m in range(members):
-        loc[1 + 2 * m].wait()
         loc[2 + 2 * m].wait()
+        loc[3 + 2 * m].wait()
+        for copy in d_copies[m]:
+            copy.wait()
 
         def step(i, carry):
             r = i // group_n
             g = i % group_n
             cols = pl.ds(pl.multiple_of(g * gcols, gcols), gcols)
             hs = pl.ds(r * hb, hb)
-            q = gq[hs, m, :, cols].reshape(rb, gcols).astype(F32) * (0.5 * hd ** (-0.5))
+            q = gq[m, hs, :, cols].reshape(rb, gcols).astype(F32) * (0.5 * hd ** (-0.5))
             q4 = jnp.concatenate(
                 [jnp.where(lane_head == h, q, 0.0).astype(BF16) for h in range(group)], axis=0
             )
@@ -209,7 +231,12 @@
             copy.start()
             f_copies.append(copy)
 
-    c1.wait()
+    o_copy.wait()
+    sibling = hist + 1 - 2 * lax.rem(hist, 2)
+    s_copy = remote(outw.at[other, rows], outw.at[other, rows], s_send, s_recv, hist=sibling)
+    s_copy.start()
+    for copy in c1:
+        copy.wait()
     blk = (
         lax.broadcasted_iota(jnp.int32, (gcols, gcols), 0) // hd
         == lax.broadcasted_iota(jnp.int32, (gcols, gcols), 1) // hd
@@ -243,18 +270,13 @@
     for copy in f_copies:
         copy.wait()
     attended += jnp.sum(recv[...].astype(F32), axis=1).reshape(rows_own, inner)
-    mix[0] = (layer_norm(attended) * proj[0].astype(F32).reshape(rows_own, inner)).astype(BF16)
-    m_copy = remote(mix.at[0], mix.at[1], m_send, m_recv, fsdp=other)
-    m_copy.start()
-    loc[-1].wait()
-    m_copy.wait()
-    bsend[...] = jnp.dot(mix[1], outw[...], preferred_element_type=F32)
-    b_copy = remote(bsend, branch.at[fsdp], b_send, b_recv, fsdp=other)
-    b_copy.start()
-    branch[fsdp] = jnp.dot(mix[0], outw[...], preferred_element_type=F32)
-    b_copy.wait()
-    full = jnp.concatenate([branch[0], branch[1]], axis=1)
-    x = cand_ref[...].astype(F32).reshape(rows_own, width)
+    mixed = (layer_norm(attended) * proj[0].astype(F32).reshape(rows_own, inner)).astype(BF16)
+    s_copy.wait()
+    full = jnp.concatenate(
+        [jnp.dot(mixed, outw[f], preferred_element_type=F32) for f in range(2)], axis=1
+    )
+    x3 = cand_ref[...].astype(F32)
+    x = jnp.concatenate([x3[:, m, :] for m in range(members)], axis=0)
     out_ref[...] = (x + full).astype(BF16).reshape(members, cdev, width)
 
 
@@ -290,27 +312,24 @@
         out_specs=vmem,
         scratch_shapes=[
             pltpu.VMEM(in_weight.shape, BF16),
-            pltpu.VMEM(out_weight.shape, BF16),
+            pltpu.VMEM((2,) + out_weight.shape, BF16),
             pltpu.VMEM(hist_keys.shape, BF16),
             pltpu.VMEM(hist_values.shape, BF16),
             pltpu.VMEM((2, own, width), BF16),
             pltpu.VMEM((4, members, cdev, inner), BF16),
             pltpu.VMEM((2, members, cdev, inner), BF16),
-            pltpu.VMEM((hist_n, members, cdev, inner), BF16),
+            pltpu.VMEM((members, hist_n, cdev, inner), BF16),
             pltpu.VMEM((members, hist_n, cdev, inner), BF16),
             pltpu.VMEM((members, hist_n, cdev, inner), BF16),
             pltpu.VMEM((members, heads, key_n), F32),
             pltpu.VMEM((members, hist_n, cdev, key_n), F32),
-            pltpu.VMEM((2, own, inner), BF16),
-            pltpu.VMEM((2, own, out_weight.shape[1]), F32),
-            pltpu.VMEM((own, out_weight.shape[1]), F32),
             dma((2 + 2 * members,)),
             dma(()),
             dma(()),
-            dma((2,)),
-            dma((2,)),
-            dma((peers,)),
-            dma((peers,)),
+            dma((2, members)),
+            dma((2, members)),
+            dma((members, peers)),
+            dma((members, peers)),
             dma((members, peers)),
             dma((members, peers)),
             dma(()),
@@ -322,8 +341,8 @@
             collective_id=0, has_side_effects=True, vmem_limit_bytes=56 * 1024 * 1024
         ),
     )(
-        candidates.transpose(1, 0, 2),
-        cand_items,
+        candidates,
+        cand_items.T,
         hist_keys,
         hist_values,
         hist_items,

time: 36.8 us -> 30.1 us (0.82)
  Pallas kernels: 32 us -> 28.3 us
  local copies, waits for them, and re-layouts: 4.48 us -> 1.54 us
    pallas_call x1, Pallas kernels: 32 us -> 28.3 us  [body(): pl.pallas_call(functools.partial(kernel, hist_n, cand_n), out_shape=jax.S...]
    unnamed x2 -> x0, local copies, waits for them, and re-layouts: 2.94 us -> none
where the time goes in v2:
time: 30.1 us; the launch traced here: 29.9 us
  Pallas kernels  28.3 us (94%)
  local copies, waits for them, and re-layouts  1.54 us (5%)
    pallas_call x1, Pallas kernels, body(): pl.pallas_call(functools.partial(kernel, hist_n, cand_n), out_shape=jax.S...  28.3 us
    transpose x1, local copies, waits for them, and re-layouts, body(): return out.transpose(1, 0, 2)  1.54 us

profile of v2, /device:TPU:0, one launch (start us, length us, event | category | flops | bytes accessed | tf_op | source)
XLA Modules:
  0.0 29.9 jit_solution(809825326981997603)
XLA Ops:
  0.0 28.3 %shard_map.109 = bf16[2,16,1024]{2,1,0:T(8,128)(2,1)} custom-call(bf16[16,2,1024]{2,1,0:T(2,128)(2,1)} %cand_ref.1, s32[4,256]{1,0:T(4,128)} %bitcast.6, bf16[2,1024,1024]{2,1,0:T(8,128)(2,1)} %keys_hbm.1, bf16[2,1024,1024]{2,1,0:T(8,128)(2,1)} %vals_hbm.1, s32[2,1024]{1,0:T(2,128)} %items_ref.1, s32[2,1024]{1,0:T(2,128)} %buckets_ref.1, s32[2]{0:T(128)} %len_ref.1, ...), custom_call_target="tpu_custom_call" | custom-call | tf_op jit(solution)/shard_map/pallas_call | solution.py:308
  28.3 1.5 %copy.12 = bf16[16,2,1024]{2,1,0:T(2,128)(2,1)} copy(bf16[16,2,1024]{2,0,1:T(8,128)(2,1)} %bitcast.4) | data formatting | bytes 131072 | tf_op jit(solution)/shard_map/transpose | solution.py:356

commit v3 on v2

--- a/solution.py
+++ b/solution.py
@@ -10,6 +10,8 @@
 MESH = pl.DeviceIdType.MESH
 F32 = jnp.float32
 BF16 = jnp.bfloat16
+PIECES = 4
+EARLY = 1
 NT = (((1,), (1,)), ((), ()))
 
 
@@ -104,6 +106,21 @@
     a_copy = remote(x_buf.at[0], x_buf.at[1], a_send, a_recv, fsdp=other)
     a_copy.start()
 
+    depth = inner // (2 * PIECES)
+    first = lax.rem(hist, 2) * (inner // 2)
+    pieces = [pl.ds(pl.multiple_of(first + k * depth, depth), depth) for k in range(PIECES)]
+    o_copies = [
+        remote(outw_hbm.at[r, :], outw.at[fsdp, r], o_send.at[k], o_recv.at[k], fsdp=other)
+        for k, r in enumerate(pieces)
+    ]
+    sibling = hist + 1 - 2 * lax.rem(hist, 2)
+    s_copies = [
+        remote(outw.at[other, r], outw.at[other, r], s_send.at[k], s_recv.at[k], hist=sibling)
+        for k, r in enumerate(pieces)
+    ]
+    for copy in o_copies[:EARLY]:
+        copy.start()
+
     table = table_ref[...]
     t_hi = table.astype(BF16)
     rest = table - t_hi.astype(F32)
@@ -174,13 +191,9 @@
         for copy in d_copies[m]:
             copy.start()
         gq[m, hist] = proj[2, m]
+    for copy in o_copies[EARLY:]:
+        copy.start()
     c1 = project(1)
-
-    depth = inner // 2
-    rows = pl.ds(pl.multiple_of(lax.rem(hist, 2) * depth, depth), depth)
-    w_copy.wait()
-    o_copy = remote(outw.at[fsdp, rows], outw.at[fsdp, rows], o_send, o_recv, fsdp=other)
-    o_copy.start()
 
     hb = 4 if hist_n % 4 == 0 else 1
     rb = hb * cdev
@@ -223,18 +236,17 @@
             part[m, hs, :, cols] = summed.astype(BF16).reshape(hb, cdev, gcols)
             return carry
 
-        lax.fori_loop(0, (hist_n // hb) * group_n, step, 0)
+        lax.fori_loop(0, (hist_n // hb) * group_n, step, 0, unroll=2)
         for o, peer in enumerate(peers):
             copy = remote(
                 part.at[m, peer], recv.at[m, hist], f_send.at[m, o], f_recv.at[m, o], hist=peer
             )
             copy.start()
             f_copies.append(copy)
-
-    o_copy.wait()
-    sibling = hist + 1 - 2 * lax.rem(hist, 2)
-    s_copy = remote(outw.at[other, rows], outw.at[other, rows], s_send, s_recv, hist=sibling)
-    s_copy.start()
+        for k in range(m * PIECES // members, (m + 1) * PIECES // members):
+            o_copies[k].wait()
+            s_copies[k].start()
+
     for copy in c1:
         copy.wait()
     blk = (
@@ -271,7 +283,9 @@
         copy.wait()
     attended += jnp.sum(recv[...].astype(F32), axis=1).reshape(rows_own, inner)
     mixed = (layer_norm(attended) * proj[0].astype(F32).reshape(rows_own, inner)).astype(BF16)
-    s_copy.wait()
+    for copy in s_copies:
+        copy.wait()
+    w_copy.wait()
     full = jnp.concatenate(
         [jnp.dot(mixed, outw[f], preferred_element_type=F32) for f in range(2)], axis=1
     )
@@ -332,10 +346,10 @@
             dma((members, peers)),
             dma((members, peers)),
             dma((members, peers)),
-            dma(()),
-            dma(()),
-            dma(()),
-            dma(()),
+            dma((PIECES,)),
+            dma((PIECES,)),
+            dma((PIECES,)),
+            dma((PIECES,)),
         ],
         compiler_params=pltpu.CompilerParams(
             collective_id=0, has_side_effects=True, vmem_limit_bytes=56 * 1024 * 1024

time: 30.1 us -> 26.4 us (0.88)
  Pallas kernels: 28.3 us -> 24.7 us
    pallas_call x1, Pallas kernels: 28.3 us -> 24.7 us  [body(): pl.pallas_call(functools.partial(kernel, hist_n, cand_n), out_shape=jax.S...]
where the time goes in v3:
time: 26.4 us; the launch traced here: 26.2 us
  Pallas kernels  24.7 us (94%)
  local copies, waits for them, and re-layouts  1.54 us (6%)
    pallas_call x1, Pallas kernels, body(): pl.pallas_call(functools.partial(kernel, hist_n, cand_n), out_shape=jax.S...  24.7 us
    transpose x1, local copies, waits for them, and re-layouts, body(): return out.transpose(1, 0, 2)  1.54 us

profile of v3, /device:TPU:0, one launch (start us, length us, event | category | flops | bytes accessed | tf_op | source)
XLA Modules:
  0.0 26.2 jit_solution(417763780713914556)
XLA Ops:
  0.0 24.7 %shard_map.109 = bf16[2,16,1024]{2,1,0:T(8,128)(2,1)} custom-call(bf16[16,2,1024]{2,1,0:T(2,128)(2,1)} %cand_ref.1, s32[4,256]{1,0:T(4,128)} %bitcast.6, bf16[2,1024,1024]{2,1,0:T(8,128)(2,1)} %keys_hbm.1, bf16[2,1024,1024]{2,1,0:T(8,128)(2,1)} %vals_hbm.1, s32[2,1024]{1,0:T(2,128)} %items_ref.1, s32[2,1024]{1,0:T(2,128)} %buckets_ref.1, s32[2]{0:T(128)} %len_ref.1, ...), custom_call_target="tpu_custom_call" | custom-call | tf_op jit(solution)/shard_map/pallas_call | solution.py:322
  24.7 1.5 %copy.12 = bf16[16,2,1024]{2,1,0:T(2,128)(2,1)} copy(bf16[16,2,1024]{2,0,1:T(8,128)(2,1)} %bitcast.4) | data formatting | bytes 131072 | tf_op jit(solution)/shard_map/transpose | solution.py:370

commit v4 on v3

--- a/solution.py
+++ b/solution.py
@@ -108,11 +108,22 @@
 
     depth = inner // (2 * PIECES)
     first = lax.rem(hist, 2) * (inner // 2)
-    pieces = [pl.ds(pl.multiple_of(first + k * depth, depth), depth) for k in range(PIECES)]
+    pair = lax.rem(hist // 2, 2)
+    pieces = [
+        pl.ds(pl.multiple_of(first + k * depth, depth), depth)
+        for k in (pair, *range(2, PIECES), 1 - pair)
+    ]
     o_copies = [
         remote(outw_hbm.at[r, :], outw.at[fsdp, r], o_send.at[k], o_recv.at[k], fsdp=other)
-        for k, r in enumerate(pieces)
+        for k, r in enumerate(pieces[:-1])
     ]
+    x_copy = remote(
+        outw.at[other, pieces[0]],
+        outw.at[other, pieces[0]],
+        o_send.at[PIECES - 1],
+        o_recv.at[PIECES - 1],
+        hist=hist + 2 - 4 * pair,
+    )
     sibling = hist + 1 - 2 * lax.rem(hist, 2)
     s_copies = [
         remote(outw.at[other, r], outw.at[other, r], s_send.at[k], s_recv.at[k], hist=sibling)
@@ -205,6 +216,10 @@
         loc[3 + 2 * m].wait()
         for copy in d_copies[m]:
             copy.wait()
+        if m == 0:
+            o_copies[0].wait()
+            x_copy.start()
+            s_copies[0].start()
 
         def step(i, carry):
             r = i // group_n
@@ -243,10 +258,11 @@
             )
             copy.start()
             f_copies.append(copy)
-        for k in range(m * PIECES // members, (m + 1) * PIECES // members):
-            o_copies[k].wait()
-            s_copies[k].start()
-
+    for k in range(1, PIECES - 1):
+        o_copies[k].wait()
+        s_copies[k].start()
+    x_copy.wait()
+    s_copies[-1].start()
     for copy in c1:
         copy.wait()
     blk = (

time: 26.4 us -> 25.5 us (0.966)
  Pallas kernels: 24.7 us -> 23.7 us
    pallas_call x1, Pallas kernels: 24.7 us -> 23.7 us  [body(): pl.pallas_call(functools.partial(kernel, hist_n, cand_n), out_shape=jax.S...]
where the time goes in v4:
time: 25.5 us; the launch traced here: 25.3 us
  Pallas kernels  23.7 us (93%)
  local copies, waits for them, and re-layouts  1.54 us (6%)
    pallas_call x1, Pallas kernels, body(): pl.pallas_call(functools.partial(kernel, hist_n, cand_n), out_shape=jax.S...  23.7 us
    transpose x1, local copies, waits for them, and re-layouts, body(): return out.transpose(1, 0, 2)  1.54 us

profile of v4, /device:TPU:0, one launch (start us, length us, event | category | flops | bytes accessed | tf_op | source)
XLA Modules:
  0.0 25.3 jit_solution(2265512053919591370)
XLA Ops:
  0.0 23.7 %shard_map.109 = bf16[2,16,1024]{2,1,0:T(8,128)(2,1)} custom-call(bf16[16,2,1024]{2,1,0:T(2,128)(2,1)} %cand_ref.1, s32[4,256]{1,0:T(4,128)} %bitcast.6, bf16[2,1024,1024]{2,1,0:T(8,128)(2,1)} %keys_hbm.1, bf16[2,1024,1024]{2,1,0:T(8,128)(2,1)} %vals_hbm.1, s32[2,1024]{1,0:T(2,128)} %items_ref.1, s32[2,1024]{1,0:T(2,128)} %buckets_ref.1, s32[2]{0:T(128)} %len_ref.1, ...), custom_call_target="tpu_custom_call" | custom-call | tf_op jit(solution)/shard_map/pallas_call | solution.py:338
  23.8 1.5 %copy.12 = bf16[16,2,1024]{2,1,0:T(2,128)(2,1)} copy(bf16[16,2,1024]{2,0,1:T(8,128)(2,1)} %bitcast.4) | data formatting | bytes 131072 | tf_op jit(solution)/shard_map/transpose | solution.py:386
